TPU v7x, 512 devices: a whole 4x8x8 slice. The times are simulated.
512 devices in a mesh: seq: 128 (over y_lo, x, z), head: 4 (over y_hi, core).
Axes of the slice: x: 4, y: 8 (y_hi: 2, y_lo: 4; y = y_hi * 4 + y_lo), z: 8, core: 2. Of those that a mesh axis runs over, the one named last changes fastest.
Arguments:
- queries: bfloat16 [32768, 32, 128], P('seq', 'head'), may hold values from -10 to 10
- out_gradient: bfloat16 [32768, 32, 128], P('seq', 'head'), may hold values from -6 to 6
- codebook: bfloat16 [2, 2048, 128], replicated, may hold values from -4 to 4
- code_ids: int32 [4, 2, 32768], P('head', None, 'seq'), may hold values from 0 to 2047
- reach_back: int32 [32768], P('seq'), may hold values from 1 to 768
Outputs:
- codebook_gradient: float32 [2, 2048, 128], P(None, ('seq', 'head'))
All inputs are finite; a program needn't handle non-finite values.
Results may differ from a plain program's by a relative error of at most 0.007.
Values may be sent and summed in bfloat16 or wider, within the bound.
A program may use at most 64 MiB of HBM per device.

v0:
```python
import math

import jax
import jax.numpy as jnp
from jax import lax
from jax.sharding import PartitionSpec as P

STEPS = 3


def from_behind(block, axis, distance):
    devices = range(lax.axis_size(axis))
    route = [(i - distance, i) for i in devices if i - distance in devices]
    return lax.ppermute(block, axis, route)


def on_device(queries, out_gradient, codebook, code_ids, reach_back):
    rows_dev, heads_dev, head_width = queries.shape
    pairs_dev = code_ids.shape[0]
    group_size = heads_dev // pairs_dev
    words_all = codebook.shape[1]
    my_index = lax.axis_index("seq")
    score_scale = 1.0 / math.sqrt(head_width)
    query_grouped = queries.reshape(rows_dev, pairs_dev, group_size, head_width)
    cotangent_grouped = out_gradient.reshape(rows_dev, pairs_dev, group_size, head_width)
    query_places = my_index * rows_dev + jnp.arange(rows_dev, dtype=jnp.int32)
    word_index = jnp.arange(words_all, dtype=jnp.int32)
    lookup = (code_ids[..., None] == word_index).astype(jnp.bfloat16)
    current = jnp.einsum(
        "gstc,scd->gstd", lookup, codebook, preferred_element_type=jnp.float32
    ).astype(jnp.bfloat16)
    held_blocks = [current]
    held_codes = [code_ids]
    for offset in range(1, STEPS + 1):
        current = from_behind(current, "seq", 1)
        held_blocks.append(current)
        held_codes.append(code_ids)

    def block_scores(offset):
        key_places = (my_index - offset) * rows_dev + jnp.arange(rows_dev, dtype=jnp.int32)
        distance = query_places[:, None] - key_places[None, :]
        allowed = (key_places[None, :] >= 0) & (distance >= 0) & (distance < reach_back[:, None])
        scores = (
            jnp.einsum(
                "tgjd,gkd->gjtk",
                query_grouped,
                held_blocks[offset][:, 0],
                preferred_element_type=jnp.float32,
            )
            * score_scale
        )
        return (allowed, scores)

    allowed, scores = block_scores(0)
    masked = jnp.where(allowed, scores, -jnp.inf)
    row_max = jnp.max(masked, axis=-1, keepdims=True)
    row_total = jnp.sum(jnp.exp(masked - row_max), axis=-1, keepdims=True)
    for offset in range(1, STEPS + 1):
        allowed, scores = block_scores(offset)
        masked = jnp.where(allowed, scores, -jnp.inf)
        new_max = jnp.maximum(row_max, jnp.max(masked, axis=-1, keepdims=True))
        row_total = row_total * jnp.exp(row_max - new_max) + jnp.sum(
            jnp.exp(masked - new_max), axis=-1, keepdims=True
        )
        row_max = new_max
    log_norm = row_max + jnp.log(row_total)

    def block_terms(offset):
        allowed, scores = block_scores(offset)
        soft_probs = jnp.where(allowed, jnp.exp(scores - log_norm), 0.0)
        dot_part = jnp.einsum(
            "tgjd,gkd->gjtk",
            cotangent_grouped,
            held_blocks[offset][:, 1],
            preferred_element_type=jnp.float32,
        )
        return (soft_probs, dot_part)

    dot_total = 0.0
    for offset in range(STEPS + 1):
        soft_probs, dot_part = block_terms(offset)
        dot_total = dot_total + jnp.sum(soft_probs * dot_part, axis=-1, keepdims=True)
    gradients = []
    for offset in range(STEPS + 1):
        soft_probs, dot_part = block_terms(offset)
        soft_weights = soft_probs.astype(jnp.bfloat16)
        score_gradient = (soft_probs * (dot_part - dot_total) * score_scale).astype(jnp.bfloat16)
        key_gradient = jnp.einsum(
            "gjtk,tgjd->gkd", score_gradient, query_grouped, preferred_element_type=jnp.float32
        )
        value_gradient = jnp.einsum(
            "gjtk,tgjd->gkd", soft_weights, cotangent_grouped, preferred_element_type=jnp.float32
        )
        gradients.append(jnp.stack([key_gradient, value_gradient], axis=1))
    carried = gradients[STEPS]
    for offset in range(STEPS - 1, -1, -1):
        carried = from_behind(carried, "seq", -1) + gradients[offset]
    lookup = (code_ids[..., None] == word_index).astype(jnp.bfloat16)
    upper = lax.optimization_barrier(carried.astype(jnp.bfloat16))
    lower = (carried - upper.astype(jnp.float32)).astype(jnp.bfloat16)
    upper_sum = jnp.einsum("gstc,gstd->scd", lookup, upper, preferred_element_type=jnp.float32)
    lower_sum = jnp.einsum("gstc,gstd->scd", lookup, lower, preferred_element_type=jnp.float32)
    partial_value = upper_sum + lower_sum
    return lax.psum_scatter(partial_value, ("seq", "head"), scatter_dimension=1, tiled=True)


def solution(mesh):
    in_specs = (
        P("seq", "head", None),
        P("seq", "head", None),
        P(),
        P("head", None, "seq"),
        P("seq"),
    )
    out_specs = P(None, ("seq", "head"), None)
    return jax.shard_map(
        on_device, mesh=mesh, in_specs=in_specs, out_specs=out_specs, check_vma=False
    )
```

profile of v0, /device:TPU:1, one launch (start us, length us, event | category | flops | bytes accessed | tf_op | source)
XLA Modules:
  0.0 380.8 jit_solution(6495484836408341779)
XLA Ops:
  6.5 1.2 copy-done
  7.8 2.0 fusion.36
  9.8 5.0 %collective-permute-start = (bf16[1,2,256,128]{3,2,1,0:T(8,128)(2,1)S(1)}, bf16[1,2,256,128]{3,2,1,0:T(8,128)(2,1)S(1)}, u32[]{:S(2)}, u32[]{:S(2)}) collective-permute-start(bf16[1,2,256,128]{3,2,1,0:T(8,128)(2,1)S(1)} %fusion.36), channel_id=1, source_target_pairs={{0,4},{4,8},{8,12},{12,16},{16,20},{20,24},{24,28},{28,32},{32,36}... | collective-permute-start | bytes 393224 | tf_op jit(solution)/shard_map/ppermute | solution.py:14
  15.3 0.5 fusion.82
  15.9 0.5 fusion.32
  16.8 4.0 %collective-permute-start.1 = (bf16[1,2,256,128]{3,2,1,0:T(8,128)(2,1)S(1)}, bf16[1,2,256,128]{3,2,1,0:T(8,128)(2,1)S(1)}, u32[]{:S(2)}, u32[]{:S(2)}) collective-permute-start(bf16[1,2,256,128]{3,2,1,0:T(8,128)(2,1)S(1)} %collective-permute-done), channel_id=1, source_target_pairs={{0,4},{4,8},{8,12},{12,16},{16,20},{20,24},{24,28},{28,32},{32,36}... | collective-permute-start | bytes 393224 | tf_op jit(solution)/shard_map/ppermute | solution.py:14
  20.9 0.5 fusion.33
  21.4 1.4 collective-permute-done.1
  22.8 4.3 %collective-permute-start.2 = (bf16[1,2,256,128]{3,2,1,0:T(8,128)(2,1)S(1)}, bf16[1,2,256,128]{3,2,1,0:T(8,128)(2,1)S(1)}, u32[]{:S(2)}, u32[]{:S(2)}) collective-permute-start(bf16[1,2,256,128]{3,2,1,0:T(8,128)(2,1)S(1)} %collective-permute-done.1), channel_id=1, source_target_pairs={{0,4},{4,8},{8,12},{12,16},{16,20},{20,24},{24,28},{28,32},{32,36}... | collective-permute-start | bytes 393224 | tf_op jit(solution)/shard_map/ppermute | solution.py:14
  27.1 0.5 fusion.34
  28.0 0.8 collective-permute-done.2
  28.8 0.5 fusion.31
  29.8 0.9 exponential_reduce_fusion
  31.1 2.7 fusion.8
  33.9 0.9 convolution_bitcast_fusion.1
  34.8 0.9 convolution_bitcast_fusion.5
  35.7 1.0 convolution_bitcast_fusion.7
  36.6 0.6 convolution_bitcast_fusion.6
  37.2 1.0 convolution_bitcast_fusion.3
  38.2 1.3 collective-permute-start.3
  39.5 0.6 convolution_bitcast_fusion.4
  40.1 7.0 %collective-permute-done.3 = f32[1,2,256,128]{3,2,1,0:T(8,128)S(1)} collective-permute-done((f32[1,2,256,128]{3,2,1,0:T(8,128)S(1)}, f32[1,2,256,128]{3,2,1,0:T(8,128)S(1)}, u32[]{:S(2)}, u32[]{:S(2)}) %collective-permute-start.3) | collective-permute-done | bytes 262176 | tf_op jit(solution)/shard_map/ppermute | solution.py:14
  47.1 1.3 collective-permute-start.4
  48.4 0.6 convolution_bitcast_fusion.2
  49.0 7.2 %collective-permute-done.4 = f32[1,2,256,128]{3,2,1,0:T(8,128)S(1)} collective-permute-done((f32[1,2,256,128]{3,2,1,0:T(8,128)S(1)}, f32[1,2,256,128]{3,2,1,0:T(8,128)S(1)}, u32[]{:S(2)}, u32[]{:S(2)}) %collective-permute-start.4) | collective-permute-done | bytes 262176 | tf_op jit(solution)/shard_map/ppermute | solution.py:14
  56.2 1.3 collective-permute-start.5
  57.5 0.6 convolution_bitcast_fusion
  58.1 6.8 %collective-permute-done.5 = f32[1,2,256,128]{3,2,1,0:T(8,128)S(1)} collective-permute-done((f32[1,2,256,128]{3,2,1,0:T(8,128)S(1)}, f32[1,2,256,128]{3,2,1,0:T(8,128)S(1)}, u32[]{:S(2)}, u32[]{:S(2)}) %collective-permute-start.5) | collective-permute-done | bytes 262176 | tf_op jit(solution)/shard_map/ppermute | solution.py:14
  65.0 0.8 fusion
  65.8 2.1 fusion.3
  67.9 304.8 %all-reduce.3.cloned.1.call-done = f32[2,2048,128]{2,1,0:T(8,128)} async-done(((f32[2,2048,128]{2,1,0:T(8,128)}), f32[2,2048,128]{2,1,0:T(8,128)}) %all-reduce.3.cloned.1.call-update) | async-done | bytes 2097168
  372.7 1.3 constant_dynamic-slice_fusion
  (32 shorter events, 2.5 us)
Async XLA Ops:
  6.5 1.2 copy-start
  6.5 8.3 %copy-start.1 = (bf16[256,8,128]{2,1,0:T(8,128)(2,1)S(1)}, bf16[256,8,128]{2,1,0:T(8,128)(2,1)}, u32[]{:S(2)}) copy-start(bf16[256,8,128]{2,1,0:T(8,128)(2,1)} %param.6) | copy-start | bytes 1572868
  6.5 366.1 %all-reduce.3.cloned.1.call-start = ((), (), s32[]{:S(2)}) async-start(), calls=%async_computation | async-start | bytes 4194304
  7.8 7.6 %copy-start.4 = (s32[256]{0:T(256)S(1)}, s32[256]{0:T(256)}, u32[]{:S(2)}) copy-start(s32[256]{0:T(256)} %param.9) | copy-start | bytes 3076
  9.8 6.1 %copy-start.2 = (bf16[256,8,128]{2,1,0:T(8,128)(2,1)S(1)}, bf16[256,8,128]{2,1,0:T(8,128)(2,1)}, u32[]{:S(2)}) copy-start(bf16[256,8,128]{2,1,0:T(8,128)(2,1)} %param.5) | copy-start | bytes 1572868
  9.8 7.0 %collective-permute-start = (bf16[1,2,256,128]{3,2,1,0:T(8,128)(2,1)S(1)}, bf16[1,2,256,128]{3,2,1,0:T(8,128)(2,1)S(1)}, u32[]{:S(2)}, u32[]{:S(2)}) collective-permute-start(bf16[1,2,256,128]{3,2,1,0:T(8,128)(2,1)S(1)} %fusion.36), channel_id=1, source_target_pairs={{0,4},{4,8},{8,12},{12,16},{16,20},{20,24},{24,28},{28,32},{32,36}... | collective-permute-start | bytes 393224 | tf_op jit(solution)/shard_map/ppermute | solution.py:14
  16.8 6.0 %collective-permute-start.1 = (bf16[1,2,256,128]{3,2,1,0:T(8,128)(2,1)S(1)}, bf16[1,2,256,128]{3,2,1,0:T(8,128)(2,1)S(1)}, u32[]{:S(2)}, u32[]{:S(2)}) collective-permute-start(bf16[1,2,256,128]{3,2,1,0:T(8,128)(2,1)S(1)} %collective-permute-done), channel_id=1, source_target_pairs={{0,4},{4,8},{8,12},{12,16},{16,20},{20,24},{24,28},{28,32},{32,36}... | collective-permute-start | bytes 393224 | tf_op jit(solution)/shard_map/ppermute | solution.py:14
  22.8 6.0 %collective-permute-start.2 = (bf16[1,2,256,128]{3,2,1,0:T(8,128)(2,1)S(1)}, bf16[1,2,256,128]{3,2,1,0:T(8,128)(2,1)S(1)}, u32[]{:S(2)}, u32[]{:S(2)}) collective-permute-start(bf16[1,2,256,128]{3,2,1,0:T(8,128)(2,1)S(1)} %collective-permute-done.1), channel_id=1, source_target_pairs={{0,4},{4,8},{8,12},{12,16},{16,20},{20,24},{24,28},{28,32},{32,36}... | collective-permute-start | bytes 393224 | tf_op jit(solution)/shard_map/ppermute | solution.py:14
  38.2 8.9 %collective-permute-start.3 = (f32[1,2,256,128]{3,2,1,0:T(8,128)S(1)}, f32[1,2,256,128]{3,2,1,0:T(8,128)S(1)}, u32[]{:S(2)}, u32[]{:S(2)}) collective-permute-start(f32[1,2,256,128]{3,2,1,0:T(8,128)S(1)} %pad_maximum_fusion), channel_id=1, source_target_pairs={{4,0},{8,4},{12,8},{16,12},{20,16},{24,20},{28,24},{32,28},{36,32}... | collective-permute-start | bytes 786440 | tf_op jit(solution)/shard_map/ppermute | solution.py:14
  47.1 9.1 %collective-permute-start.4 = (f32[1,2,256,128]{3,2,1,0:T(8,128)S(1)}, f32[1,2,256,128]{3,2,1,0:T(8,128)S(1)}, u32[]{:S(2)}, u32[]{:S(2)}) collective-permute-start(f32[1,2,256,128]{3,2,1,0:T(8,128)S(1)} %maximum_add_fusion), channel_id=1, source_target_pairs={{4,0},{8,4},{12,8},{16,12},{20,16},{24,20},{28,24},{32,28},{36,32}... | collective-permute-start | bytes 786440 | tf_op jit(solution)/shard_map/ppermute | solution.py:14
  56.2 8.8 %copy-start.3 = (s32[1,2,256]{2,1,0:T(2,128)S(1)}, s32[1,2,256]{2,1,0:T(2,128)}, u32[]{:S(2)}) copy-start(s32[1,2,256]{2,1,0:T(2,128)} %param.8) | copy-start | bytes 6148
  56.2 8.7 %collective-permute-start.5 = (f32[1,2,256,128]{3,2,1,0:T(8,128)S(1)}, f32[1,2,256,128]{3,2,1,0:T(8,128)S(1)}, u32[]{:S(2)}, u32[]{:S(2)}) collective-permute-start(f32[1,2,256,128]{3,2,1,0:T(8,128)S(1)} %maximum_add_fusion.1), channel_id=1, source_target_pairs={{4,0},{8,4},{12,8},{16,12},{20,16},{24,20},{28,24},{32,28},{36,32}... | collective-permute-start | bytes 786440 | tf_op jit(solution)/shard_map/ppermute | solution.py:14
Sparse Core Ops, SparseCore 0:
  68.0 304.5 all-reduce.2
where the time goes:
time: 381 us
  waiting for transfers between devices  328 us (86%)
  starting transfers between devices  17.2 us (5%)
  matrix products  16.8 us (4%)
  between operations  13.7 us (4%)
    unnamed x2, waiting for transfers between devices  305 us
    ppermute x6, waiting for transfers between devices, from_behind(): return lax.ppermute(block, axis, route)  23.3 us
    ppermute x6, starting transfers between devices, from_behind(): return lax.ppermute(block, axis, route)  17.2 us
  transfers between devices with their start and end apart: 7, of which 6 were waited for; matrix products, arithmetic and copies ran while one was open for 1% of the time, Pallas kernels for 0%

commit v1 on v0

v1 whole, which is shorter than its diff:
```python
import math

import jax
import jax.numpy as jnp
from jax import lax
from jax.experimental import pallas as pl
from jax.experimental.pallas import tpu as pltpu
from jax.sharding import PartitionSpec as P

MESH = pl.DeviceIdType.MESH
SPAN = 768
XN, YLO, YHI, ZN = 4, 4, 2, 8
YN = YLO * YHI
F32, BF16 = jnp.float32, jnp.bfloat16


def nn(a, b):
    return lax.dot_general(a, b, (((1,), (0,)), ((), ())), preferred_element_type=F32)


def nt(a, b):
    return lax.dot_general(a, b, (((1,), (1,)), ((), ())), preferred_element_type=F32)


def split_halves(a, b):
    low = lax.broadcasted_iota(jnp.int32, a.shape, 1) < 4
    return (
        jnp.where(low, a, pltpu.roll(b, 4, 1)),
        jnp.where(low, pltpu.roll(a, 4, 1), b),
    )


def kernel(
    q_ref, g_ref, cb_ref, ids_ref, reach_ref, out_ref,
    cbt, onehot, rows, grads, low_ref, ids_all, keep, csend, crecv, xsend, xrecv, xown,
    ysend, yrecv, yred, zsend, zrecv,
    id_s, id_r, c_s, c_r, x_s, x_r, y_s, y_r, z_s, z_r,
):
    tok = reach_ref.shape[1]
    words, width = cb_ref.shape[1], cb_ref.shape[2]
    n_rows = q_ref.shape[0]
    group = n_rows // tok
    blocks = SPAN // tok + 1
    scale = 1.0 / math.sqrt(width)
    seq, head = lax.axis_index("seq"), lax.axis_index("head")
    n_seq = lax.axis_size("seq")
    z = seq % ZN
    x = (seq // ZN) % XN
    y_lo = seq // (ZN * XN)
    y_hi, core = head // 2, head % 2
    y = y_hi * YLO + y_lo

    def device(x_at, y_at, z_at, core_at):
        return (((y_at % YLO) * XN + x_at) * ZN + z_at, (y_at // YLO) * 2 + core_at)

    buddy = device(x, y, z, 1 - core)
    x_peers = [device((x + i) % XN, y, z, core) for i in range(1, XN)]
    y_peers = [device(x, (y + i) % YN, z, core) for i in range(1, YN)]
    z_peers = [device(x, y, (z + i) % ZN, core) for i in range(1, ZN)]
    ahead = [((seq + i) % n_seq, head) for i in range(1, blocks)]
    behind = [((seq + n_seq - i) % n_seq, head) for i in range(1, blocks)]

    barrier = pltpu.get_barrier_semaphore()
    greeted = [buddy] + x_peers + y_peers + z_peers + behind
    for peer in greeted:
        pl.semaphore_signal(barrier, inc=1, device_id=peer, device_id_type=MESH)

    seg = words // 16
    for s in range(16):
        base = (s % YLO) * (seg * XN) + (s // YLO) * seg
        for table in range(2):
            cbt[table, :, s * seg : (s + 1) * seg] = cb_ref[table, base : base + seg, :].T

    tiles = 8
    tile_tok = tok // tiles
    lanes = tile_tok * group
    place = seq * tok + lax.broadcasted_iota(jnp.int32, (1, tok), 1)
    reach = jnp.minimum(reach_ref[...], place + 1)
    at_tile = lax.broadcasted_iota(jnp.int32, (tiles, tok), 1) // tile_tok == lax.broadcasted_iota(
        jnp.int32, (tiles, tok), 0
    )
    spread = (
        lax.broadcasted_iota(jnp.int32, (tok, lanes), 0) % tile_tok
        == lax.broadcasted_iota(jnp.int32, (tok, lanes), 1) // group
    ).astype(F32).astype(BF16)

    def expand(part):
        return nn(jnp.where(at_tile, part.astype(F32), 0.0).astype(BF16), spread)

    tau = lax.broadcasted_iota(jnp.int32, (1, lanes), 1) // group
    reach_wide = (expand(reach // 256) * 256.0 + expand(reach % 256)).astype(jnp.int32)
    low_ref[...] = SPAN + tau - reach_wide

    ids_all[blocks - 1] = ids_ref[...]
    grads[...] = jnp.zeros_like(grads)

    pl.semaphore_wait(barrier, len(greeted))

    id_copies = []
    for i in range(blocks - 1):
        copy = pltpu.make_async_remote_copy(
            src_ref=ids_ref,
            dst_ref=ids_all.at[blocks - 2 - i],
            send_sem=id_s.at[i],
            recv_sem=id_r.at[i],
            device_id=ahead[i],
            device_id_type=MESH,
        )
        copy.start()
        id_copies.append(copy)

    def decode(block):
        cols = slice(block * tok, (block + 1) * tok)
        for table in range(2):
            ids = ids_all[block, table : table + 1, :]
            for s in range(16):
                base = (s % YLO) * (seg * XN) + (s // YLO) * seg
                word = base + lax.broadcasted_iota(jnp.int32, (seg, tok), 0)
                onehot[table, s * seg : (s + 1) * seg, cols] = (
                    (word == ids).astype(F32).astype(BF16)
                )
            rows[table, cols, :] = nn(cbt[table], onehot[table, :, cols]).T.astype(BF16)

    decode(blocks - 1)
    for i in range(blocks - 1):
        id_copies[i].wait()
    for block in range(blocks - 1):
        decode(block)

    win = SPAN + tile_tok

    def tile_step(a, carry):
        at = pl.ds(pl.multiple_of(a * lanes, lanes), lanes)
        keys = pl.ds(pl.multiple_of(a * tile_tok, tile_tok), win)
        q, g = q_ref[at, :], g_ref[at, :]
        low = low_ref[pl.ds(a, 1), :]
        index = lax.broadcasted_iota(jnp.int32, (win, lanes), 0)
        allowed = (index > low) & (index <= SPAN + tau)
        s = jnp.where(allowed, nt(rows[0, keys, :], q), -1e30)
        top = jnp.max(s, axis=0, keepdims=True)
        c = scale * math.log2(math.e)
        p = jnp.exp2((s - top) * c)
        inv = 1.0 / jnp.sum(p, axis=0, keepdims=True)
        d = nt(rows[1, keys, :], g)
        total = jnp.sum(p * d, axis=0, keepdims=True) * inv
        w = p * inv
        e = (w * (d - total) * scale).astype(BF16)
        grads[0, keys, :] += nn(e, q)
        grads[1, keys, :] += nn(w.astype(BF16), g)
        return carry

    lax.fori_loop(0, tiles, tile_step, 0)

    half = words // XN // 2
    upper = [grads[table].astype(BF16) for table in range(2)]
    order = (2, 1, 3, 0)
    c_copies = {}
    for i in order:
        x_to = (x + i) % XN
        for table in range(2):
            at = pl.ds(pl.multiple_of(x_to * (words // XN), words // XN), words // XN)
            part = nn(onehot[table, at, :], upper[table]).reshape(half // 8, 16, width)
            first, second = split_halves(part[:, :8, :], part[:, 8:, :])
            first, second = first.reshape(half, width), second.reshape(half, width)
            keep[i, table * half : (table + 1) * half, :] = jnp.where(core == 0, first, second)
            csend[i, table * half : (table + 1) * half, :] = jnp.where(
                core == 0, second, first
            ).astype(BF16)
        copy = pltpu.make_async_remote_copy(
            src_ref=csend.at[i],
            dst_ref=crecv.at[i],
            send_sem=c_s.at[i],
            recv_sem=c_r.at[i],
            device_id=buddy,
            device_id_type=MESH,
        )
        copy.start()
        c_copies[i] = copy

    x_copies = []
    for i in order:
        c_copies[i].wait()
        chip = keep[i] + crecv[i].astype(F32)
        if i == 0:
            xown[...] = chip
            continue
        xsend[i - 1] = chip.astype(BF16)
        copy = pltpu.make_async_remote_copy(
            src_ref=xsend.at[i - 1],
            dst_ref=xrecv.at[i - 1],
            send_sem=x_s.at[i - 1],
            recv_sem=x_r.at[i - 1],
            device_id=x_peers[i - 1],
            device_id_type=MESH,
        )
        copy.start()
        x_copies.append(copy)
    for copy in x_copies:
        copy.wait()

    line = xown[...]
    for i in range(XN - 1):
        line = line + xrecv[i].astype(F32)
    line = line.reshape(2, half // 8, 8, width)
    for at_hi, part in enumerate(split_halves(line[0], line[1])):
        yred[at_hi * YLO : (at_hi + 1) * YLO] = part.reshape(YLO, ZN * 8, width)
    ysend[...] = yred[...].astype(BF16)
    y_copies = []
    for i in range(1, YN):
        copy = pltpu.make_async_remote_copy(
            src_ref=ysend.at[(y + i) % YN],
            dst_ref=yrecv.at[i - 1],
            send_sem=y_s.at[i - 1],
            recv_sem=y_r.at[i - 1],
            device_id=y_peers[i - 1],
            device_id_type=MESH,
        )
        copy.start()
        y_copies.append(copy)
    for copy in y_copies:
        copy.wait()
    plane = yred[y]
    for i in range(YN - 1):
        plane = plane + yrecv[i].astype(F32)
    zsend[...] = plane.reshape(ZN, 8, width)
    z_copies = []
    for i in range(1, ZN):
        copy = pltpu.make_async_remote_copy(
            src_ref=zsend.at[(z + i) % ZN],
            dst_ref=zrecv.at[i - 1],
            send_sem=z_s.at[i - 1],
            recv_sem=z_r.at[i - 1],
            device_id=z_peers[i - 1],
            device_id_type=MESH,
        )
        copy.start()
        z_copies.append(copy)
    for copy in z_copies:
        copy.wait()
    done = zsend[z]
    for i in range(ZN - 1):
        done = done + zrecv[i]
    out_ref[...] = done


def on_device(queries, out_gradient, codebook, code_ids, reach_back):
    tok, heads, width = queries.shape
    words = codebook.shape[1]
    blocks = SPAN // tok + 1
    half = words // XN // 2
    dma = pltpu.SemaphoreType.DMA
    out = pl.pallas_call(
        kernel,
        out_shape=jax.ShapeDtypeStruct((8, width), F32),
        in_specs=[pl.BlockSpec(memory_space=pltpu.VMEM)] * 5,
        out_specs=pl.BlockSpec(memory_space=pltpu.VMEM),
        scratch_shapes=[
            pltpu.VMEM((2, width, words), BF16),
            pltpu.VMEM((2, words, blocks * tok), BF16),
            pltpu.VMEM((2, blocks * tok, width), BF16),
            pltpu.VMEM((2, blocks * tok, width), F32),
            pltpu.VMEM((8, tok), jnp.int32),
            pltpu.VMEM((blocks, 2, tok), jnp.int32),
            pltpu.VMEM((XN, 2 * half, width), F32),
            pltpu.VMEM((XN, 2 * half, width), BF16),
            pltpu.VMEM((XN, 2 * half, width), BF16),
            pltpu.VMEM((XN - 1, 2 * half, width), BF16),
            pltpu.VMEM((XN - 1, 2 * half, width), BF16),
            pltpu.VMEM((2 * half, width), F32),
            pltpu.VMEM((YN, ZN * 8, width), BF16),
            pltpu.VMEM((YN - 1, ZN * 8, width), BF16),
            pltpu.VMEM((YN, ZN * 8, width), F32),
            pltpu.VMEM((ZN, 8, width), F32),
            pltpu.VMEM((ZN - 1, 8, width), F32),
            dma((blocks - 1,)), dma((blocks - 1,)),
            dma((XN,)), dma((XN,)),
            dma((XN - 1,)), dma((XN - 1,)),
            dma((YN - 1,)), dma((YN - 1,)),
            dma((ZN - 1,)), dma((ZN - 1,)),
        ],
        compiler_params=pltpu.CompilerParams(
            collective_id=0, has_side_effects=True, vmem_limit_bytes=48 * 2**20
        ),
    )(
        queries.reshape(tok * heads, width),
        out_gradient.reshape(tok * heads, width),
        codebook,
        code_ids.reshape(2, tok),
        reach_back.reshape(1, tok),
    )
    return out.reshape(2, 4, width)


def solution(mesh):
    in_specs = (
        P("seq", "head", None),
        P("seq", "head", None),
        P(),
        P("head", None, "seq"),
        P("seq"),
    )
    out_specs = P(None, ("seq", "head"), None)
    return jax.shard_map(
        on_device, mesh=mesh, in_specs=in_specs, out_specs=out_specs, check_vma=False
    )
```

time: 381 us -> 55.1 us (0.14)
  waiting for transfers between devices: 328 us -> 0 us
  Pallas kernels: 0 us -> 50 us
  starting transfers between devices: 17.2 us -> 0 us
  matrix products: 16.8 us -> 0 us
  between operations: 13.7 us -> 0.01 us
    unnamed x2 -> x0, waiting for transfers between devices: 305 us -> none
    pallas_call x0 -> x1, Pallas kernels: none -> 50 us  [on_device(): pl.pallas_call(kernel, out_shape=jax.ShapeDtypeStruct((8, width), F32), i...]
    ppermute x6 -> x0, waiting for transfers between devices: 23.3 us -> none  [from_behind(): return lax.ppermute(block, axis, route)]
    ppermute x6 -> x0, starting transfers between devices: 17.2 us -> none  [from_behind(): return lax.ppermute(block, axis, route)]
    dot_general x19 -> x0, matrix products: 16.8 us -> none  [the longest x4 4 us: block_terms(): jnp.einsum('tgjd,gkd->gjtk', cotangent_grouped, held_blocks[offset][:, 1]...]
  transfers between devices with their start and end apart: 7 -> 0, of which waited for: 6 -> 0; matrix products, arithmetic and copies ran while one was open for 1% -> 0% of each run, Pallas kernels for 0% -> 0%
where the time goes in v1:
time: 55.1 us; the launch traced here: 54.6 us
  Pallas kernels  50 us (91%)
  local copies, waits for them, and re-layouts  4.59 us (8%)
    pallas_call x1, Pallas kernels, on_device(): pl.pallas_call(kernel, out_shape=jax.ShapeDtypeStruct((8, width), F32), i...  50 us
    unnamed x11, local copies, waits for them, and re-layouts  4.59 us

profile of v1, /device:TPU:1, one launch (start us, length us, event | category | flops | bytes accessed | tf_op | source)
XLA Modules:
  0.0 54.6 jit_solution(13761952801557129516)
XLA Ops:
  0.0 0.0 copy-start.3
  0.0 0.0 copy-start.4
  0.0 0.7 %copy-done.3 = s32[1,2,256]{2,1,0:T(2,128)S(1)} copy-done((s32[1,2,256]{2,1,0:T(2,128)S(1)}, s32[1,2,256]{2,1,0:T(2,128)}, u32[]{:S(2)}) %copy-start.3) | copy-done | bytes 2072
  0.7 0.0 copy-done.4
  0.7 0.0 copy-start
  0.7 1.2 %copy-done = bf16[2,2048,128]{2,1,0:T(8,128)(2,1)S(1)} copy-done((bf16[2,2048,128]{2,1,0:T(8,128)(2,1)S(1)}, bf16[2,2048,128]{2,1,0:T(8,128)(2,1)}, u32[]{:S(2)}) %copy-start) | copy-done | bytes 1048600
  1.9 0.0 copy-start.1
  1.9 1.0 %copy-done.1 = bf16[256,8,128]{2,1,0:T(8,128)(2,1)S(1)} copy-done((bf16[256,8,128]{2,1,0:T(8,128)(2,1)S(1)}, bf16[256,8,128]{2,1,0:T(8,128)(2,1)}, u32[]{:S(2)}) %copy-start.1) | copy-done | bytes 524312
  3.0 0.0 copy-start.2
  3.0 1.0 %copy-done.2 = bf16[256,8,128]{2,1,0:T(8,128)(2,1)S(1)} copy-done((bf16[256,8,128]{2,1,0:T(8,128)(2,1)S(1)}, bf16[256,8,128]{2,1,0:T(8,128)(2,1)}, u32[]{:S(2)}) %copy-start.2) | copy-done | bytes 524312
  4.0 50.0 %shard_map.55 = f32[8,128]{1,0:T(8,128)S(1)} custom-call(bf16[2048,128]{1,0:T(8,128)(2,1)S(1)} %bitcast.5, bf16[2048,128]{1,0:T(8,128)(2,1)S(1)} %bitcast.6, bf16[2,2048,128]{2,1,0:T(8,128)(2,1)S(1)} %copy-done, s32[2,256]{1,0:T(2,128)S(1)} %bitcast.8, s32[1,256]{1,0:T(1,128)S(1)} %bitcast.9), custom_call_target="tpu_custom_call" | custom-call | tf_op jit(solution)/shard_map/pallas_call | solution.py:252
  54.0 0.6 %copy.7 = f32[2,4,128]{2,1,0:T(4,128)} copy(f32[2,4,128]{2,1,0:T(4,128)S(1)} %bitcast.7) | data formatting | bytes 8192
Async XLA Ops:
  0.0 0.7 %copy-start.3 = (s32[1,2,256]{2,1,0:T(2,128)S(1)}, s32[1,2,256]{2,1,0:T(2,128)}, u32[]{:S(2)}) copy-start(s32[1,2,256]{2,1,0:T(2,128)} %param.8) | copy-start | bytes 6148
  0.0 0.7 %copy-start.4 = (s32[256]{0:T(256)S(1)}, s32[256]{0:T(256)}, u32[]{:S(2)}) copy-start(s32[256]{0:T(256)} %param.9) | copy-start | bytes 3076
  0.7 1.2 %copy-start = (bf16[2,2048,128]{2,1,0:T(8,128)(2,1)S(1)}, bf16[2,2048,128]{2,1,0:T(8,128)(2,1)}, u32[]{:S(2)}) copy-start(bf16[2,2048,128]{2,1,0:T(8,128)(2,1)} %cb_ref.1) | copy-start | bytes 3145732
  1.9 1.0 %copy-start.1 = (bf16[256,8,128]{2,1,0:T(8,128)(2,1)S(1)}, bf16[256,8,128]{2,1,0:T(8,128)(2,1)}, u32[]{:S(2)}) copy-start(bf16[256,8,128]{2,1,0:T(8,128)(2,1)} %param.5) | copy-start | bytes 1572868
  3.0 1.0 %copy-start.2 = (bf16[256,8,128]{2,1,0:T(8,128)(2,1)S(1)}, bf16[256,8,128]{2,1,0:T(8,128)(2,1)}, u32[]{:S(2)}) copy-start(bf16[256,8,128]{2,1,0:T(8,128)(2,1)} %param.6) | copy-start | bytes 1572868

commit v2 on v1

v2 whole, which is shorter than its diff:
```python
import math

import jax
import jax.numpy as jnp
from jax import lax
from jax.experimental import pallas as pl
from jax.experimental.pallas import tpu as pltpu
from jax.sharding import PartitionSpec as P

MESH = pl.DeviceIdType.MESH
SPAN = 768
XN, YLO, YHI, ZN = 4, 4, 2, 8
YN = YLO * YHI
HIGH, LOW = 8, 256
TILES = 8
F32, BF16 = jnp.float32, jnp.bfloat16


def nn(a, b):
    return lax.dot_general(a, b, (((1,), (0,)), ((), ())), preferred_element_type=F32)


def nt(a, b):
    return lax.dot_general(a, b, (((1,), (1,)), ((), ())), preferred_element_type=F32)


def split_halves(a, b):
    low = lax.broadcasted_iota(jnp.int32, a.shape, 1) < 4
    return (
        jnp.where(low, a, pltpu.roll(b, 4, 1)),
        jnp.where(low, pltpu.roll(a, 4, 1), b),
    )


def kernel(
    q_hbm, g_hbm, cb_hbm, ids_hbm, reach_hbm, out_ref,
    q_ref, g_ref, cb_ref, reach_ref, ids_all,
    cbt, onehot, high, rows, grads, low_ref, part_ref,
    keep, csend, crecv, xsend, xrecv, ysend, yrecv, yred, zsend, zrecv,
    in_s, id_s, id_r, c_s, c_r, x_s, x_r, y_s, y_r, z_s, z_r,
):
    tok = reach_ref.shape[1]
    words, width = cb_ref.shape[1], cb_ref.shape[2]
    n_rows = q_ref.shape[0]
    group = n_rows // tok
    blocks = SPAN // tok + 1
    scale = 1.0 / math.sqrt(width)
    seq, head = lax.axis_index("seq"), lax.axis_index("head")
    n_seq = lax.axis_size("seq")
    z = seq % ZN
    x = (seq // ZN) % XN
    x_hi, x_lo = x // 2, x % 2
    y_lo = seq // (ZN * XN)
    y_hi, core = head // 2, head % 2
    y = y_hi * YLO + y_lo

    def device(x_at, y_at, z_at, core_at):
        return (((y_at % YLO) * XN + x_at) * ZN + z_at, (y_at // YLO) * 2 + core_at)

    def x_other(j):
        hi = 1 - x_hi if j // 2 else x_hi
        lo = 1 - x_lo if j % 2 else x_lo
        return hi * 2 + lo

    buddy = device(x, y, z, 1 - core)
    x_peers = [device(x_other(j), y, z, core) for j in range(1, XN)]
    y_peers = [device(x, (y + i) % YN, z, core) for i in range(1, YN)]
    z_peers = [device(x, y, (z + i) % ZN, core) for i in range(1, ZN)]
    ahead = [((seq + i) % n_seq, head) for i in range(1, blocks)]
    behind = [((seq + n_seq - i) % n_seq, head) for i in range(1, blocks)]

    barrier = pltpu.get_barrier_semaphore()
    greeted = [buddy] + x_peers + y_peers + z_peers + behind
    for peer in greeted:
        pl.semaphore_signal(barrier, inc=1, device_id=peer, device_id_type=MESH)

    loads = [
        pltpu.make_async_copy(src, dst, in_s.at[i])
        for i, (src, dst) in enumerate(
            (
                (ids_hbm, ids_all.at[blocks - 1]),
                (reach_hbm, reach_ref),
                (cb_hbm, cb_ref),
                (q_hbm, q_ref),
                (g_hbm, g_ref),
            )
        )
    ]
    for load in loads:
        load.start()
    grads[...] = jnp.zeros_like(grads)

    tile_tok = tok // TILES
    lanes = tile_tok * group
    tau = lax.broadcasted_iota(jnp.int32, (1, lanes), 1) // group
    at_tile = lax.broadcasted_iota(jnp.int32, (TILES, tok), 1) // tile_tok == lax.broadcasted_iota(
        jnp.int32, (TILES, tok), 0
    )
    spread = (
        lax.broadcasted_iota(jnp.int32, (tok, lanes), 0) % tile_tok
        == lax.broadcasted_iota(jnp.int32, (tok, lanes), 1) // group
    ).astype(F32).astype(BF16)

    def expand(part):
        return nn(jnp.where(at_tile, part.astype(F32), 0.0).astype(BF16), spread)

    loads[0].wait()
    loads[1].wait()
    place = seq * tok + lax.broadcasted_iota(jnp.int32, (1, tok), 1)
    reach = jnp.minimum(reach_ref[...], place + 1)
    reach_wide = (expand(reach // 256) * 256.0 + expand(reach % 256)).astype(jnp.int32)
    low_ref[...] = SPAN + tau - reach_wide

    loads[2].wait()
    for table in range(2):
        for h in range(HIGH):
            cbt[table, h * width : (h + 1) * width, :] = cb_ref[
                table, h * LOW : (h + 1) * LOW, :
            ].T

    pl.semaphore_wait(barrier, len(greeted))

    id_copies = []
    for i in range(blocks - 1):
        copy = pltpu.make_async_remote_copy(
            src_ref=ids_all.at[blocks - 1],
            dst_ref=ids_all.at[blocks - 2 - i],
            send_sem=id_s.at[i],
            recv_sem=id_r.at[i],
            device_id=ahead[i],
            device_id_type=MESH,
        )
        copy.start()
        id_copies.append(copy)

    def decode(block):
        cols = slice(block * tok, (block + 1) * tok)
        ids = ids_all[block]
        hi = ids // LOW
        columns = jnp.concatenate(
            [hi.astype(F32), jnp.zeros((6, tok), F32)], axis=0
        ).T
        word = lax.broadcasted_iota(jnp.int32, (LOW, tok), 0)
        for table in range(2):
            onehot[table, :, cols] = (
                (word == ids[table : table + 1, :] % LOW).astype(F32).astype(BF16)
            )
            high[table, cols, :] = jnp.broadcast_to(
                columns[:, table : table + 1], (tok, width)
            ).astype(BF16)
            found = nn(cbt[table], onehot[table, :, cols])
            own = found[:width]
            for h in range(1, HIGH):
                own = jnp.where(
                    hi[table : table + 1, :] == h, found[h * width : (h + 1) * width], own
                )
            rows[table, cols, :] = own.T.astype(BF16)

    decode(blocks - 1)
    for load in loads[3:]:
        load.wait()
    for i in range(blocks - 1):
        id_copies[i].wait()
        decode(blocks - 2 - i)

    win = SPAN + tile_tok

    def tile_step(a, carry):
        at = pl.ds(pl.multiple_of(a * lanes, lanes), lanes)
        keys = pl.ds(pl.multiple_of(a * tile_tok, tile_tok), win)
        q, g = q_ref[at, :], g_ref[at, :]
        low = low_ref[pl.ds(a, 1), :]
        index = lax.broadcasted_iota(jnp.int32, (win, lanes), 0)
        s = jnp.where(index > low, nt(rows[0, keys, :], q), -1e30)
        last = jnp.where(index[:tile_tok] <= tau, s[SPAN:], -1e30)
        s = jnp.concatenate([s[:SPAN], last], axis=0)
        top = jnp.max(s, axis=0, keepdims=True)
        p = jnp.exp2((s - top) * (scale * math.log2(math.e)))
        inv = 1.0 / jnp.sum(p, axis=0, keepdims=True)
        d = nt(rows[1, keys, :], g)
        total = jnp.sum(p * d, axis=0, keepdims=True) * inv
        e = ((p * (inv * scale)) * (d - total)).astype(BF16)
        w = (p * inv).astype(BF16)
        grads[0, keys, :] += nn(e, q)
        grads[1, keys, :] += nn(w, g)
        return carry

    lax.fori_loop(0, TILES, tile_step, 0, unroll=2)

    half = words // XN // 2
    y_rows = half // YLO
    c_copies = {}
    for flip in (1, 0):
        at_hi = 1 - x_hi if flip else x_hi
        for table in range(2):
            part = grads[table].astype(BF16)
            wide = jnp.concatenate(
                [
                    jnp.where(
                        high[table] == (at_y * 2 + at_hi).astype(F32).astype(BF16),
                        part,
                        jnp.zeros_like(part),
                    )
                    for at_y in range(YLO)
                ],
                axis=1,
            )
            part_ref[table] = nn(onehot[table], wide)
        for j in (flip * 2 + 1, flip * 2):
            at_lo = 1 - x_lo if j % 2 else x_lo
            span = pl.ds(pl.multiple_of(at_lo * (LOW // 2), LOW // 2), LOW // 2)
            for table in range(2):
                for at_y in range(YLO):
                    part = part_ref[table, span, at_y * width : (at_y + 1) * width]
                    part = part.reshape(LOW // 32, 16, width)
                    first, second = split_halves(part[:, :8, :], part[:, 8:, :])
                    first, second = first.reshape(y_rows, width), second.reshape(y_rows, width)
                    to = slice(table * half + at_y * y_rows, table * half + (at_y + 1) * y_rows)
                    keep[j, to, :] = jnp.where(core == 0, first, second)
                    csend[j, to, :] = jnp.where(core == 0, second, first).astype(BF16)
            copy = pltpu.make_async_remote_copy(
                src_ref=csend.at[j],
                dst_ref=crecv.at[j],
                send_sem=c_s.at[j],
                recv_sem=c_r.at[j],
                device_id=buddy,
                device_id_type=MESH,
            )
            copy.start()
            c_copies[j] = copy

    x_copies = []
    for j in (3, 2, 1):
        c_copies[j].wait()
        xsend[j - 1] = (keep[j] + crecv[j].astype(F32)).astype(BF16)
        copy = pltpu.make_async_remote_copy(
            src_ref=xsend.at[j - 1],
            dst_ref=xrecv.at[j - 1],
            send_sem=x_s.at[j - 1],
            recv_sem=x_r.at[j - 1],
            device_id=x_peers[j - 1],
            device_id_type=MESH,
        )
        copy.start()
        x_copies.append(copy)
    c_copies[0].wait()
    for copy in x_copies:
        copy.wait()

    line = keep[0] + crecv[0].astype(F32)
    for i in range(XN - 1):
        line = line + xrecv[i].astype(F32)
    line = line.reshape(2, half // 8, 8, width)
    for at_hi, part in enumerate(split_halves(line[0], line[1])):
        yred[at_hi * YLO : (at_hi + 1) * YLO] = part.reshape(YLO, ZN * 8, width)
    ysend[...] = yred[...].astype(BF16)
    y_copies = []
    for i in range(1, YN):
        copy = pltpu.make_async_remote_copy(
            src_ref=ysend.at[(y + i) % YN],
            dst_ref=yrecv.at[i - 1],
            send_sem=y_s.at[i - 1],
            recv_sem=y_r.at[i - 1],
            device_id=y_peers[i - 1],
            device_id_type=MESH,
        )
        copy.start()
        y_copies.append(copy)
    for copy in y_copies:
        copy.wait()
    plane = yred[y]
    for i in range(YN - 1):
        plane = plane + yrecv[i].astype(F32)
    zsend[...] = plane.reshape(ZN, 8, width)
    z_copies = []
    for i in range(1, ZN):
        copy = pltpu.make_async_remote_copy(
            src_ref=zsend.at[(z + i) % ZN],
            dst_ref=zrecv.at[i - 1],
            send_sem=z_s.at[i - 1],
            recv_sem=z_r.at[i - 1],
            device_id=z_peers[i - 1],
            device_id_type=MESH,
        )
        copy.start()
        z_copies.append(copy)
    for copy in z_copies:
        copy.wait()
    done = zsend[z]
    for i in range(ZN - 1):
        done = done + zrecv[i]
    out_ref[...] = done


def on_device(queries, out_gradient, codebook, code_ids, reach_back):
    tok, heads, width = queries.shape
    words = codebook.shape[1]
    blocks = SPAN // tok + 1
    half = words // XN // 2
    dma = pltpu.SemaphoreType.DMA
    out = pl.pallas_call(
        kernel,
        out_shape=jax.ShapeDtypeStruct((8, width), F32),
        in_specs=[pl.BlockSpec(memory_space=pl.ANY)] * 5,
        out_specs=pl.BlockSpec(memory_space=pltpu.VMEM),
        scratch_shapes=[
            pltpu.VMEM((tok * heads, width), BF16),
            pltpu.VMEM((tok * heads, width), BF16),
            pltpu.VMEM((2, words, width), BF16),
            pltpu.VMEM((1, tok), jnp.int32),
            pltpu.VMEM((blocks, 2, tok), jnp.int32),
            pltpu.VMEM((2, HIGH * width, LOW), BF16),
            pltpu.VMEM((2, LOW, blocks * tok), BF16),
            pltpu.VMEM((2, blocks * tok, width), BF16),
            pltpu.VMEM((2, blocks * tok, width), BF16),
            pltpu.VMEM((2, blocks * tok, width), F32),
            pltpu.VMEM((TILES, tok), jnp.int32),
            pltpu.VMEM((2, LOW, YLO * width), F32),
            pltpu.VMEM((XN, 2 * half, width), F32),
            pltpu.VMEM((XN, 2 * half, width), BF16),
            pltpu.VMEM((XN, 2 * half, width), BF16),
            pltpu.VMEM((XN - 1, 2 * half, width), BF16),
            pltpu.VMEM((XN - 1, 2 * half, width), BF16),
            pltpu.VMEM((YN, ZN * 8, width), BF16),
            pltpu.VMEM((YN - 1, ZN * 8, width), BF16),
            pltpu.VMEM((YN, ZN * 8, width), F32),
            pltpu.VMEM((ZN, 8, width), F32),
            pltpu.VMEM((ZN - 1, 8, width), F32),
            dma((5,)),
            dma((blocks - 1,)), dma((blocks - 1,)),
            dma((XN,)), dma((XN,)),
            dma((XN - 1,)), dma((XN - 1,)),
            dma((YN - 1,)), dma((YN - 1,)),
            dma((ZN - 1,)), dma((ZN - 1,)),
        ],
        compiler_params=pltpu.CompilerParams(
            collective_id=0, has_side_effects=True, vmem_limit_bytes=56 * 2**20
        ),
    )(
        queries.reshape(tok * heads, width),
        out_gradient.reshape(tok * heads, width),
        codebook,
        code_ids.reshape(2, tok),
        reach_back.reshape(1, tok),
    )
    return out.reshape(2, 4, width)


def solution(mesh):
    in_specs = (
        P("seq", "head", None),
        P("seq", "head", None),
        P(),
        P("head", None, "seq"),
        P("seq"),
    )
    out_specs = P(None, ("seq", "head"), None)
    return jax.shard_map(
        on_device, mesh=mesh, in_specs=in_specs, out_specs=out_specs, check_vma=False
    )
```

time: 55.1 us -> 51 us (0.926)
  local copies, waits for them, and re-layouts: 4.59 us -> 1.28 us
  Pallas kernels: 50 us -> 49.2 us
    unnamed x11 -> x1, local copies, waits for them, and re-layouts: 4.59 us -> 1.28 us
    pallas_call x1, Pallas kernels: 50 us -> 49.2 us  [on_device(): pl.pallas_call(kernel, out_shape=jax.ShapeDtypeStruct((8, width), F32), i...]
where the time goes in v2:
time: 51 us; the launch traced here: 50.5 us
  Pallas kernels  49.2 us (96%)
  local copies, waits for them, and re-layouts  1.28 us (3%)
    pallas_call x1, Pallas kernels, on_device(): pl.pallas_call(kernel, out_shape=jax.ShapeDtypeStruct((8, width), F32), i...  49.2 us
    unnamed x1, local copies, waits for them, and re-layouts  1.28 us

profile of v2, /device:TPU:1, one launch (start us, length us, event | category | flops | bytes accessed | tf_op | source)
XLA Modules:
  0.0 50.5 jit_solution(12827992548952048685)
XLA Ops:
  0.0 49.2 %shard_map.55 = f32[8,128]{1,0:T(8,128)} custom-call(bf16[2048,128]{1,0:T(8,128)(2,1)} %bitcast.5, bf16[2048,128]{1,0:T(8,128)(2,1)} %bitcast.6, bf16[2,2048,128]{2,1,0:T(8,128)(2,1)} %cb_hbm.1, s32[2,256]{1,0:T(2,128)} %bitcast.8, s32[1,256]{1,0:T(1,128)} %bitcast.9), custom_call_target="tpu_custom_call" | custom-call | tf_op jit(solution)/shard_map/pallas_call | solution.py:301
  49.2 1.3 %copy.7 = f32[2,4,128]{2,1,0:T(4,128)} copy(f32[2,4,128]{2,1,0:T(4,128)} %bitcast.7) | data formatting | bytes 8192

commit v3 on v2

--- a/solution.py
+++ b/solution.py
@@ -35,7 +35,7 @@
 def kernel(
     q_hbm, g_hbm, cb_hbm, ids_hbm, reach_hbm, out_ref,
     q_ref, g_ref, cb_ref, reach_ref, ids_all,
-    cbt, onehot, high, rows, grads, low_ref, part_ref,
+    cbt, onehot, high, rows, grads, low_ref, part_ref, s_ref, d_ref, e_ref, w_ref,
     keep, csend, crecv, xsend, xrecv, ysend, yrecv, yred, zsend, zrecv,
     in_s, id_s, id_r, c_s, c_r, x_s, x_r, y_s, y_r, z_s, z_r,
 ):
@@ -70,7 +70,7 @@
     behind = [((seq + n_seq - i) % n_seq, head) for i in range(1, blocks)]
 
     barrier = pltpu.get_barrier_semaphore()
-    greeted = [buddy] + x_peers + y_peers + z_peers + behind
+    greeted = behind + z_peers + y_peers + x_peers + [buddy]
     for peer in greeted:
         pl.semaphore_signal(barrier, inc=1, device_id=peer, device_id_type=MESH)
 
@@ -164,98 +164,152 @@
         decode(blocks - 2 - i)
 
     win = SPAN + tile_tok
-
-    def tile_step(a, carry):
-        at = pl.ds(pl.multiple_of(a * lanes, lanes), lanes)
-        keys = pl.ds(pl.multiple_of(a * tile_tok, tile_tok), win)
-        q, g = q_ref[at, :], g_ref[at, :]
-        low = low_ref[pl.ds(a, 1), :]
-        index = lax.broadcasted_iota(jnp.int32, (win, lanes), 0)
-        s = jnp.where(index > low, nt(rows[0, keys, :], q), -1e30)
-        last = jnp.where(index[:tile_tok] <= tau, s[SPAN:], -1e30)
-        s = jnp.concatenate([s[:SPAN], last], axis=0)
-        top = jnp.max(s, axis=0, keepdims=True)
-        p = jnp.exp2((s - top) * (scale * math.log2(math.e)))
-        inv = 1.0 / jnp.sum(p, axis=0, keepdims=True)
-        d = nt(rows[1, keys, :], g)
-        total = jnp.sum(p * d, axis=0, keepdims=True) * inv
-        e = ((p * (inv * scale)) * (d - total)).astype(BF16)
-        w = (p * inv).astype(BF16)
-        grads[0, keys, :] += nn(e, q)
-        grads[1, keys, :] += nn(w, g)
-        return carry
-
-    lax.fori_loop(0, TILES, tile_step, 0, unroll=2)
+    step = tile_tok
+    steps = win // step
+    ramp = lax.broadcasted_iota(jnp.int32, (step, lanes), 0)
+    inverse = {}
+
+    def queries_of(a):
+        return slice(a * lanes, (a + 1) * lanes)
+
+    def keys_of(a):
+        return slice(a * tile_tok, a * tile_tok + win)
+
+    def part_of(j):
+        return slice(j * step, (j + 1) * step)
+
+    def softmax(a):
+        low = low_ref[a : a + 1, :] - ramp
+        top = None
+        for j in range(steps):
+            s = jnp.where(low < j * step, s_ref[a, part_of(j), :], -1e30)
+            if j == steps - 1:
+                s = jnp.where(ramp <= tau, s, -1e30)
+            s_ref[a, part_of(j), :] = s
+            top = s if j == 0 else jnp.maximum(top, s)
+        top = jnp.max(top, axis=0, keepdims=True)
+        norm = jnp.zeros((step, lanes), F32)
+        for j in range(steps):
+            p = jnp.exp2((s_ref[a, part_of(j), :] - top) * (scale * math.log2(math.e)))
+            s_ref[a, part_of(j), :] = p
+            norm = norm + p
+        inverse[a] = 1.0 / jnp.sum(norm, axis=0, keepdims=True)
+        for j in range(steps):
+            w_ref[a % 2, part_of(j), :] = (s_ref[a, part_of(j), :] * inverse[a]).astype(BF16)
+
+    def score_gradient(a):
+        total = jnp.zeros((step, lanes), F32)
+        for j in range(steps):
+            total = total + s_ref[a, part_of(j), :] * d_ref[a % 2, part_of(j), :]
+        total = jnp.sum(total, axis=0, keepdims=True) * inverse[a]
+        factor = inverse[a] * scale
+        for j in range(steps):
+            p, d = s_ref[a, part_of(j), :], d_ref[a % 2, part_of(j), :]
+            e_ref[a % 2, part_of(j), :] = ((p * factor) * (d - total)).astype(BF16)
+
+    def add_values(a):
+        grads[1, keys_of(a), :] += nn(w_ref[a % 2], g_ref[queries_of(a), :])
+
+    def add_keys(a):
+        grads[0, keys_of(a), :] += nn(e_ref[a % 2], q_ref[queries_of(a), :])
 
     half = words // XN // 2
     y_rows = half // YLO
-    c_copies = {}
-    for flip in (1, 0):
+    c_copies, x_copies = {}, {}
+
+    def scatter(table, flip):
         at_hi = 1 - x_hi if flip else x_hi
-        for table in range(2):
-            part = grads[table].astype(BF16)
-            wide = jnp.concatenate(
-                [
-                    jnp.where(
-                        high[table] == (at_y * 2 + at_hi).astype(F32).astype(BF16),
-                        part,
-                        jnp.zeros_like(part),
-                    )
-                    for at_y in range(YLO)
-                ],
-                axis=1,
-            )
-            part_ref[table] = nn(onehot[table], wide)
+        part = grads[table].astype(BF16)
+        wide = jnp.concatenate(
+            [
+                jnp.where(
+                    high[table] == (at_y * 2 + at_hi).astype(F32).astype(BF16),
+                    part,
+                    jnp.zeros_like(part),
+                )
+                for at_y in range(YLO)
+            ],
+            axis=1,
+        )
+        part_ref[table] = nn(onehot[table], wide)
+
+    def to_buddy(table, flip):
         for j in (flip * 2 + 1, flip * 2):
             at_lo = 1 - x_lo if j % 2 else x_lo
             span = pl.ds(pl.multiple_of(at_lo * (LOW // 2), LOW // 2), LOW // 2)
-            for table in range(2):
-                for at_y in range(YLO):
-                    part = part_ref[table, span, at_y * width : (at_y + 1) * width]
-                    part = part.reshape(LOW // 32, 16, width)
-                    first, second = split_halves(part[:, :8, :], part[:, 8:, :])
-                    first, second = first.reshape(y_rows, width), second.reshape(y_rows, width)
-                    to = slice(table * half + at_y * y_rows, table * half + (at_y + 1) * y_rows)
-                    keep[j, to, :] = jnp.where(core == 0, first, second)
-                    csend[j, to, :] = jnp.where(core == 0, second, first).astype(BF16)
+            for at_y in range(YLO):
+                part = part_ref[table, span, at_y * width : (at_y + 1) * width]
+                part = part.reshape(LOW // 32, 16, width)
+                first, second = split_halves(part[:, :8, :], part[:, 8:, :])
+                first, second = first.reshape(y_rows, width), second.reshape(y_rows, width)
+                to = slice(at_y * y_rows, (at_y + 1) * y_rows)
+                keep[table, j, to, :] = jnp.where(core == 0, first, second)
+                csend[table, j, to, :] = jnp.where(core == 0, second, first).astype(BF16)
             copy = pltpu.make_async_remote_copy(
-                src_ref=csend.at[j],
-                dst_ref=crecv.at[j],
-                send_sem=c_s.at[j],
-                recv_sem=c_r.at[j],
+                src_ref=csend.at[table, j],
+                dst_ref=crecv.at[table, j],
+                send_sem=c_s.at[table, j],
+                recv_sem=c_r.at[table, j],
                 device_id=buddy,
                 device_id_type=MESH,
             )
             copy.start()
-            c_copies[j] = copy
-
-    x_copies = []
-    for j in (3, 2, 1):
-        c_copies[j].wait()
-        xsend[j - 1] = (keep[j] + crecv[j].astype(F32)).astype(BF16)
+            c_copies[table, j] = copy
+
+    def to_x(table, j):
+        c_copies[table, j].wait()
+        xsend[table, j - 1] = (keep[table, j] + crecv[table, j].astype(F32)).astype(BF16)
         copy = pltpu.make_async_remote_copy(
-            src_ref=xsend.at[j - 1],
-            dst_ref=xrecv.at[j - 1],
-            send_sem=x_s.at[j - 1],
-            recv_sem=x_r.at[j - 1],
+            src_ref=xsend.at[table, j - 1],
+            dst_ref=xrecv.at[table, j - 1],
+            send_sem=x_s.at[table, j - 1],
+            recv_sem=x_r.at[table, j - 1],
             device_id=x_peers[j - 1],
             device_id_type=MESH,
         )
         copy.start()
-        x_copies.append(copy)
-    c_copies[0].wait()
-    for copy in x_copies:
-        copy.wait()
-
-    line = keep[0] + crecv[0].astype(F32)
-    for i in range(XN - 1):
-        line = line + xrecv[i].astype(F32)
-    line = line.reshape(2, half // 8, 8, width)
-    for at_hi, part in enumerate(split_halves(line[0], line[1])):
+        x_copies[table, j] = copy
+
+    def chip_line(table):
+        c_copies[table, 0].wait()
+        total = keep[table, 0] + crecv[table, 0].astype(F32)
+        for j in (3, 2, 1):
+            x_copies[table, j].wait()
+            total = total + xrecv[table, j - 1].astype(F32)
+        return total.reshape(half // 8, 8, width)
+
+    for a in range(TILES):
+        s_ref[a] = nt(rows[0, keys_of(a), :], q_ref[queries_of(a), :])
+        if a > 0:
+            add_values(a - 1)
+        softmax(a)
+    add_values(TILES - 1)
+    for flip in (1, 0):
+        scatter(1, flip)
+        to_buddy(1, flip)
+    for a in range(TILES):
+        d_ref[a % 2] = nt(rows[1, keys_of(a), :], g_ref[queries_of(a), :])
+        if a > 0:
+            add_keys(a - 1)
+        if a == 3:
+            for j in (3, 2, 1):
+                to_x(1, j)
+        score_gradient(a)
+    add_keys(TILES - 1)
+    scatter(0, 1)
+    to_buddy(0, 1)
+    scatter(0, 0)
+    to_x(0, 3)
+    to_x(0, 2)
+    to_buddy(0, 0)
+    to_x(0, 1)
+    value_line = chip_line(1)
+    key_line = chip_line(0)
+    for at_hi, part in enumerate(split_halves(key_line, value_line)):
         yred[at_hi * YLO : (at_hi + 1) * YLO] = part.reshape(YLO, ZN * 8, width)
     ysend[...] = yred[...].astype(BF16)
     y_copies = []
-    for i in range(1, YN):
+    for i in (4, 3, 5, 2, 6, 1, 7):
         copy = pltpu.make_async_remote_copy(
             src_ref=ysend.at[(y + i) % YN],
             dst_ref=yrecv.at[i - 1],
@@ -273,7 +327,7 @@
         plane = plane + yrecv[i].astype(F32)
     zsend[...] = plane.reshape(ZN, 8, width)
     z_copies = []
-    for i in range(1, ZN):
+    for i in (4, 3, 5, 2, 6, 1, 7):
         copy = pltpu.make_async_remote_copy(
             src_ref=zsend.at[(z + i) % ZN],
             dst_ref=zrecv.at[i - 1],
@@ -301,7 +355,7 @@
     out = pl.pallas_call(
         kernel,
         out_shape=jax.ShapeDtypeStruct((8, width), F32),
-        in_specs=[pl.BlockSpec(memory_space=pl.ANY)] * 5,
+        in_specs=[pl.BlockSpec(memory_space=pltpu.HBM)] * 5,
         out_specs=pl.BlockSpec(memory_space=pltpu.VMEM),
         scratch_shapes=[
             pltpu.VMEM((tok * heads, width), BF16),
@@ -316,11 +370,15 @@
             pltpu.VMEM((2, blocks * tok, width), F32),
             pltpu.VMEM((TILES, tok), jnp.int32),
             pltpu.VMEM((2, LOW, YLO * width), F32),
-            pltpu.VMEM((XN, 2 * half, width), F32),
-            pltpu.VMEM((XN, 2 * half, width), BF16),
-            pltpu.VMEM((XN, 2 * half, width), BF16),
-            pltpu.VMEM((XN - 1, 2 * half, width), BF16),
-            pltpu.VMEM((XN - 1, 2 * half, width), BF16),
+            pltpu.VMEM((TILES, SPAN + tok // TILES, tok // TILES * heads), F32),
+            pltpu.VMEM((2, SPAN + tok // TILES, tok // TILES * heads), F32),
+            pltpu.VMEM((2, SPAN + tok // TILES, tok // TILES * heads), BF16),
+            pltpu.VMEM((2, SPAN + tok // TILES, tok // TILES * heads), BF16),
+            pltpu.VMEM((2, XN, half, width), F32),
+            pltpu.VMEM((2, XN, half, width), BF16),
+            pltpu.VMEM((2, XN, half, width), BF16),
+            pltpu.VMEM((2, XN - 1, half, width), BF16),
+            pltpu.VMEM((2, XN - 1, half, width), BF16),
             pltpu.VMEM((YN, ZN * 8, width), BF16),
             pltpu.VMEM((YN - 1, ZN * 8, width), BF16),
             pltpu.VMEM((YN, ZN * 8, width), F32),
@@ -328,8 +386,8 @@
             pltpu.VMEM((ZN - 1, 8, width), F32),
             dma((5,)),
             dma((blocks - 1,)), dma((blocks - 1,)),
-            dma((XN,)), dma((XN,)),
-            dma((XN - 1,)), dma((XN - 1,)),
+            dma((2, XN)), dma((2, XN)),
+            dma((2, XN - 1)), dma((2, XN - 1)),
             dma((YN - 1,)), dma((YN - 1,)),
             dma((ZN - 1,)), dma((ZN - 1,)),
         ],

time: 51 us -> 46.2 us (0.906)
  Pallas kernels: 49.2 us -> 44.3 us
    pallas_call x1, Pallas kernels: 49.2 us -> 44.3 us  [on_device(): pl.pallas_call(kernel, out_shape=jax.ShapeDtypeStruct((8, width), F32), i...]
where the time goes in v3:
time: 46.2 us; the launch traced here: 45.6 us
  Pallas kernels  44.3 us (96%)
  local copies, waits for them, and re-layouts  1.28 us (3%)
    pallas_call x1, Pallas kernels, on_device(): pl.pallas_call(kernel, out_shape=jax.ShapeDtypeStruct((8, width), F32), i...  44.3 us
    unnamed x1, local copies, waits for them, and re-layouts  1.28 us

profile of v3, /device:TPU:1, one launch (start us, length us, event | category | flops | bytes accessed | tf_op | source)
XLA Modules:
  0.0 45.6 jit_solution(11675921240554438206)
XLA Ops:
  0.0 44.3 %shard_map.55 = f32[8,128]{1,0:T(8,128)} custom-call(bf16[2048,128]{1,0:T(8,128)(2,1)} %bitcast.5, bf16[2048,128]{1,0:T(8,128)(2,1)} %bitcast.6, bf16[2,2048,128]{2,1,0:T(8,128)(2,1)} %cb_hbm.1, s32[2,256]{1,0:T(2,128)} %bitcast.8, s32[1,256]{1,0:T(1,128)} %bitcast.9), custom_call_target="tpu_custom_call" | custom-call | tf_op jit(solution)/shard_map/pallas_call | solution.py:355
  44.3 1.3 %copy.7 = f32[2,4,128]{2,1,0:T(4,128)} copy(f32[2,4,128]{2,1,0:T(4,128)} %bitcast.7) | data formatting | bytes 8192

commit v4 on v3

--- a/solution.py
+++ b/solution.py
@@ -35,9 +35,9 @@
 def kernel(
     q_hbm, g_hbm, cb_hbm, ids_hbm, reach_hbm, out_ref,
     q_ref, g_ref, cb_ref, reach_ref, ids_all,
-    cbt, onehot, high, rows, grads, low_ref, part_ref, s_ref, d_ref, e_ref, w_ref,
-    keep, csend, crecv, xsend, xrecv, ysend, yrecv, yred, zsend, zrecv,
-    in_s, id_s, id_r, c_s, c_r, x_s, x_r, y_s, y_r, z_s, z_r,
+    cbt, onehot, high, rows, grads, low_ref, own_ref, part_ref, s_ref, d_ref, e_ref, w_ref,
+    keep, csend, crecv, xsend, xrecv, yred, precv,
+    in_s, id_s, id_r, c_s, c_r, x_s, x_r, line_s, p_s, p_r,
 ):
     tok = reach_ref.shape[1]
     words, width = cb_ref.shape[1], cb_ref.shape[2]
@@ -69,6 +69,11 @@
     ahead = [((seq + i) % n_seq, head) for i in range(1, blocks)]
     behind = [((seq + n_seq - i) % n_seq, head) for i in range(1, blocks)]
 
+    offsets = sorted(
+        ((i, j) for i in range(YN) for j in range(ZN) if i or j),
+        key=lambda at: -min(at[0], YN - at[0]) - min(at[1], ZN - at[1]),
+    )
+
     barrier = pltpu.get_barrier_semaphore()
     greeted = behind + z_peers + y_peers + x_peers + [buddy]
     for peer in greeted:
@@ -132,6 +137,9 @@
         )
         copy.start()
         id_copies.append(copy)
+
+    for peer in y_peers:
+        pl.semaphore_signal(line_s, inc=1, device_id=peer, device_id_type=MESH)
 
     def decode(block):
         cols = slice(block * tok, (block + 1) * tok)
@@ -156,18 +164,11 @@
                 )
             rows[table, cols, :] = own.T.astype(BF16)
 
-    decode(blocks - 1)
-    for load in loads[3:]:
-        load.wait()
-    for i in range(blocks - 1):
-        id_copies[i].wait()
-        decode(blocks - 2 - i)
-
     win = SPAN + tile_tok
     step = tile_tok
     steps = win // step
     ramp = lax.broadcasted_iota(jnp.int32, (step, lanes), 0)
-    inverse = {}
+    inverse, shrink = {}, {}
 
     def queries_of(a):
         return slice(a * lanes, (a + 1) * lanes)
@@ -178,34 +179,66 @@
     def part_of(j):
         return slice(j * step, (j + 1) * step)
 
-    def softmax(a):
+    exponent = scale * math.log2(math.e)
+
+    def old_steps(a):
+        return range(steps - 1 - a)
+
+    def own_steps(a):
+        return range(steps - 1 - a, steps)
+
+    def masked_top(a, parts):
         low = low_ref[a : a + 1, :] - ramp
         top = None
-        for j in range(steps):
+        for j in parts:
             s = jnp.where(low < j * step, s_ref[a, part_of(j), :], -1e30)
             if j == steps - 1:
                 s = jnp.where(ramp <= tau, s, -1e30)
             s_ref[a, part_of(j), :] = s
-            top = s if j == 0 else jnp.maximum(top, s)
-        top = jnp.max(top, axis=0, keepdims=True)
+            top = s if top is None else jnp.maximum(top, s)
+        return jnp.max(top, axis=0, keepdims=True)
+
+    def exponentials(a, parts, top):
         norm = jnp.zeros((step, lanes), F32)
-        for j in range(steps):
-            p = jnp.exp2((s_ref[a, part_of(j), :] - top) * (scale * math.log2(math.e)))
+        for j in parts:
+            p = jnp.exp2((s_ref[a, part_of(j), :] - top) * exponent)
             s_ref[a, part_of(j), :] = p
             norm = norm + p
-        inverse[a] = 1.0 / jnp.sum(norm, axis=0, keepdims=True)
-        for j in range(steps):
-            w_ref[a % 2, part_of(j), :] = (s_ref[a, part_of(j), :] * inverse[a]).astype(BF16)
+        return jnp.sum(norm, axis=0, keepdims=True)
+
+    def weighted_dots(a, parts):
+        total = jnp.zeros((step, lanes), F32)
+        for j in parts:
+            total = total + s_ref[a, part_of(j), :] * d_ref[a, part_of(j), :]
+        return jnp.sum(total, axis=0, keepdims=True)
+
+    def own_part(a):
+        top = masked_top(a, own_steps(a))
+        own_ref[0, a : a + 1, :] = top
+        own_ref[1, a : a + 1, :] = exponentials(a, own_steps(a), top)
+        own_ref[2, a : a + 1, :] = weighted_dots(a, own_steps(a))
+
+    def softmax(a):
+        own_top = own_ref[0, a : a + 1, :]
+        top = jnp.maximum(masked_top(a, old_steps(a)), own_top)
+        shrink[a] = jnp.exp2((own_top - top) * exponent)
+        norm = exponentials(a, old_steps(a), top) + own_ref[1, a : a + 1, :] * shrink[a]
+        inverse[a] = 1.0 / norm
+        for parts, factor in (
+            (old_steps(a), inverse[a]),
+            (own_steps(a), inverse[a] * shrink[a]),
+        ):
+            for j in parts:
+                w_ref[a % 2, part_of(j), :] = (s_ref[a, part_of(j), :] * factor).astype(BF16)
 
     def score_gradient(a):
-        total = jnp.zeros((step, lanes), F32)
-        for j in range(steps):
-            total = total + s_ref[a, part_of(j), :] * d_ref[a % 2, part_of(j), :]
-        total = jnp.sum(total, axis=0, keepdims=True) * inverse[a]
+        total = weighted_dots(a, old_steps(a)) + own_ref[2, a : a + 1, :] * shrink[a]
+        total = total * inverse[a]
         factor = inverse[a] * scale
-        for j in range(steps):
-            p, d = s_ref[a, part_of(j), :], d_ref[a % 2, part_of(j), :]
-            e_ref[a % 2, part_of(j), :] = ((p * factor) * (d - total)).astype(BF16)
+        for parts, factor in ((old_steps(a), factor), (own_steps(a), factor * shrink[a])):
+            for j in parts:
+                p, d = s_ref[a, part_of(j), :], d_ref[a, part_of(j), :]
+                e_ref[a % 2, part_of(j), :] = ((p * factor) * (d - total)).astype(BF16)
 
     def add_values(a):
         grads[1, keys_of(a), :] += nn(w_ref[a % 2], g_ref[queries_of(a), :])
@@ -278,8 +311,23 @@
             total = total + xrecv[table, j - 1].astype(F32)
         return total.reshape(half // 8, 8, width)
 
+    decode(blocks - 1)
+    for load in loads[3:]:
+        load.wait()
     for a in range(TILES):
-        s_ref[a] = nt(rows[0, keys_of(a), :], q_ref[queries_of(a), :])
+        own = slice(SPAN - a * step, win)
+        own_keys = slice(SPAN, SPAN + (a + 1) * step)
+        s_ref[a, own, :] = nt(rows[0, own_keys, :], q_ref[queries_of(a), :])
+        d_ref[a, own, :] = nt(rows[1, own_keys, :], g_ref[queries_of(a), :])
+        own_part(a)
+    for i in range(blocks - 1):
+        id_copies[i].wait()
+        decode(blocks - 2 - i)
+
+    for a in range(TILES):
+        s_ref[a, : SPAN - a * step, :] = nt(
+            rows[0, a * step : SPAN, :], q_ref[queries_of(a), :]
+        )
         if a > 0:
             add_values(a - 1)
         softmax(a)
@@ -288,7 +336,9 @@
         scatter(1, flip)
         to_buddy(1, flip)
     for a in range(TILES):
-        d_ref[a % 2] = nt(rows[1, keys_of(a), :], g_ref[queries_of(a), :])
+        d_ref[a, : SPAN - a * step, :] = nt(
+            rows[1, a * step : SPAN, :], g_ref[queries_of(a), :]
+        )
         if a > 0:
             add_keys(a - 1)
         if a == 3:
@@ -303,46 +353,24 @@
     to_x(0, 2)
     to_buddy(0, 0)
     to_x(0, 1)
+    pl.semaphore_wait(line_s, len(y_peers))
     value_line = chip_line(1)
     key_line = chip_line(0)
     for at_hi, part in enumerate(split_halves(key_line, value_line)):
-        yred[at_hi * YLO : (at_hi + 1) * YLO] = part.reshape(YLO, ZN * 8, width)
-    ysend[...] = yred[...].astype(BF16)
-    y_copies = []
-    for i in (4, 3, 5, 2, 6, 1, 7):
+        yred[at_hi * YLO : (at_hi + 1) * YLO] = part.reshape(YLO, ZN, 8, width)
+    for slot, (i, j) in enumerate(offsets):
         copy = pltpu.make_async_remote_copy(
-            src_ref=ysend.at[(y + i) % YN],
-            dst_ref=yrecv.at[i - 1],
-            send_sem=y_s.at[i - 1],
-            recv_sem=y_r.at[i - 1],
-            device_id=y_peers[i - 1],
+            src_ref=yred.at[(y + i) % YN, (z + j) % ZN],
+            dst_ref=precv.at[slot],
+            send_sem=p_s,
+            recv_sem=p_r,
+            device_id=device(x, (y + i) % YN, (z + j) % ZN, core),
             device_id_type=MESH,
         )
         copy.start()
-        y_copies.append(copy)
-    for copy in y_copies:
-        copy.wait()
-    plane = yred[y]
-    for i in range(YN - 1):
-        plane = plane + yrecv[i].astype(F32)
-    zsend[...] = plane.reshape(ZN, 8, width)
-    z_copies = []
-    for i in (4, 3, 5, 2, 6, 1, 7):
-        copy = pltpu.make_async_remote_copy(
-            src_ref=zsend.at[(z + i) % ZN],
-            dst_ref=zrecv.at[i - 1],
-            send_sem=z_s.at[i - 1],
-            recv_sem=z_r.at[i - 1],
-            device_id=z_peers[i - 1],
-            device_id_type=MESH,
-        )
-        copy.start()
-        z_copies.append(copy)
-    for copy in z_copies:
-        copy.wait()
-    done = zsend[z]
-    for i in range(ZN - 1):
-        done = done + zrecv[i]
+    pltpu.make_async_copy(precv, precv, p_r).wait()
+    pltpu.make_async_copy(precv, precv, p_s).wait()
+    done = yred[y, z] + jnp.sum(precv[...], axis=0)
     out_ref[...] = done
 
 
@@ -369,9 +397,10 @@
             pltpu.VMEM((2, blocks * tok, width), BF16),
             pltpu.VMEM((2, blocks * tok, width), F32),
             pltpu.VMEM((TILES, tok), jnp.int32),
+            pltpu.VMEM((3, TILES, tok), F32),
             pltpu.VMEM((2, LOW, YLO * width), F32),
             pltpu.VMEM((TILES, SPAN + tok // TILES, tok // TILES * heads), F32),
-            pltpu.VMEM((2, SPAN + tok // TILES, tok // TILES * heads), F32),
+            pltpu.VMEM((TILES, SPAN + tok // TILES, tok // TILES * heads), F32),
             pltpu.VMEM((2, SPAN + tok // TILES, tok // TILES * heads), BF16),
             pltpu.VMEM((2, SPAN + tok // TILES, tok // TILES * heads), BF16),
             pltpu.VMEM((2, XN, half, width), F32),
@@ -379,17 +408,13 @@
             pltpu.VMEM((2, XN, half, width), BF16),
             pltpu.VMEM((2, XN - 1, half, width), BF16),
             pltpu.VMEM((2, XN - 1, half, width), BF16),
-            pltpu.VMEM((YN, ZN * 8, width), BF16),
-            pltpu.VMEM((YN - 1, ZN * 8, width), BF16),
-            pltpu.VMEM((YN, ZN * 8, width), F32),
-            pltpu.VMEM((ZN, 8, width), F32),
-            pltpu.VMEM((ZN - 1, 8, width), F32),
+            pltpu.VMEM((YN, ZN, 8, width), F32),
+            pltpu.VMEM((YN * ZN - 1, 8, width), F32),
             dma((5,)),
             dma((blocks - 1,)), dma((blocks - 1,)),
             dma((2, XN)), dma((2, XN)),
             dma((2, XN - 1)), dma((2, XN - 1)),
-            dma((YN - 1,)), dma((YN - 1,)),
-            dma((ZN - 1,)), dma((ZN - 1,)),
+            pltpu.SemaphoreType.REGULAR, dma, dma,
         ],
         compiler_params=pltpu.CompilerParams(
             collective_id=0, has_side_effects=True, vmem_limit_bytes=56 * 2**20

time: 46.2 us -> 45.3 us (0.981)
  Pallas kernels: 44.3 us -> 43.6 us
    pallas_call x1, Pallas kernels: 44.3 us -> 43.6 us  [on_device(): pl.pallas_call(kernel, out_shape=jax.ShapeDtypeStruct((8, width), F32), i...]
where the time goes in v4:
time: 45.3 us; the launch traced here: 44.9 us
  Pallas kernels  43.6 us (96%)
  local copies, waits for them, and re-layouts  1.28 us (3%)
    pallas_call x1, Pallas kernels, on_device(): pl.pallas_call(kernel, out_shape=jax.ShapeDtypeStruct((8, width), F32), i...  43.6 us
    unnamed x1, local copies, waits for them, and re-layouts  1.28 us

profile of v4, /device:TPU:1, one launch (start us, length us, event | category | flops | bytes accessed | tf_op | source)
XLA Modules:
  0.0 44.9 jit_solution(14279970036707838943)
XLA Ops:
  0.0 43.6 %shard_map.55 = f32[8,128]{1,0:T(8,128)} custom-call(bf16[2048,128]{1,0:T(8,128)(2,1)} %bitcast.5, bf16[2048,128]{1,0:T(8,128)(2,1)} %bitcast.6, bf16[2,2048,128]{2,1,0:T(8,128)(2,1)} %cb_hbm.1, s32[2,256]{1,0:T(2,128)} %bitcast.8, s32[1,256]{1,0:T(1,128)} %bitcast.9), custom_call_target="tpu_custom_call" | custom-call | tf_op jit(solution)/shard_map/pallas_call | solution.py:383
  43.6 1.3 %copy.7 = f32[2,4,128]{2,1,0:T(4,128)} copy(f32[2,4,128]{2,1,0:T(4,128)} %bitcast.7) | data formatting | bytes 8192

commit v5 on v4

--- a/solution.py
+++ b/solution.py
@@ -36,8 +36,8 @@
     q_hbm, g_hbm, cb_hbm, ids_hbm, reach_hbm, out_ref,
     q_ref, g_ref, cb_ref, reach_ref, ids_all,
     cbt, onehot, high, rows, grads, low_ref, own_ref, part_ref, s_ref, d_ref, e_ref, w_ref,
-    keep, csend, crecv, xsend, xrecv, yred, precv,
-    in_s, id_s, id_r, c_s, c_r, x_s, x_r, line_s, p_s, p_r,
+    keep, csend, crecv, xsend, xrecv, yred, ysend, precv,
+    in_s, id_s, id_r, c_s, c_r, x_s, x_r, near_s, two_s, line_s, p_s, p_r,
 ):
     tok = reach_ref.shape[1]
     words, width = cb_ref.shape[1], cb_ref.shape[2]
@@ -65,7 +65,19 @@
     buddy = device(x, y, z, 1 - core)
     x_peers = [device(x_other(j), y, z, core) for j in range(1, XN)]
     y_peers = [device(x, (y + i) % YN, z, core) for i in range(1, YN)]
-    z_peers = [device(x, y, (z + i) % ZN, core) for i in range(1, ZN)]
+
+    def at_distance(i):
+        return [
+            device(x, (y + i) % YN, z, core),
+            device(x, (y + YN - i) % YN, z, core),
+            device(x, y, (z + i) % ZN, core),
+            device(x, y, (z + ZN - i) % ZN, core),
+        ]
+
+    def tell(semaphore, peers):
+        for peer in peers:
+            pl.semaphore_signal(semaphore, inc=1, device_id=peer, device_id_type=MESH)
+
     ahead = [((seq + i) % n_seq, head) for i in range(1, blocks)]
     behind = [((seq + n_seq - i) % n_seq, head) for i in range(1, blocks)]
 
@@ -75,7 +87,7 @@
     )
 
     barrier = pltpu.get_barrier_semaphore()
-    greeted = behind + z_peers + y_peers + x_peers + [buddy]
+    greeted = behind + at_distance(1) + x_peers + [buddy]
     for peer in greeted:
         pl.semaphore_signal(barrier, inc=1, device_id=peer, device_id_type=MESH)
 
@@ -138,8 +150,7 @@
         copy.start()
         id_copies.append(copy)
 
-    for peer in y_peers:
-        pl.semaphore_signal(line_s, inc=1, device_id=peer, device_id_type=MESH)
+    tell(near_s, at_distance(1))
 
     def decode(block):
         cols = slice(block * tok, (block + 1) * tok)
@@ -323,6 +334,8 @@
     for i in range(blocks - 1):
         id_copies[i].wait()
         decode(blocks - 2 - i)
+    pl.semaphore_wait(near_s, 4)
+    tell(two_s, at_distance(2))
 
     for a in range(TILES):
         s_ref[a, : SPAN - a * step, :] = nt(
@@ -332,6 +345,8 @@
             add_values(a - 1)
         softmax(a)
     add_values(TILES - 1)
+    pl.semaphore_wait(two_s, 4)
+    tell(line_s, y_peers)
     for flip in (1, 0):
         scatter(1, flip)
         to_buddy(1, flip)
@@ -341,7 +356,7 @@
         )
         if a > 0:
             add_keys(a - 1)
-        if a == 3:
+        if a == 2:
             for j in (3, 2, 1):
                 to_x(1, j)
         score_gradient(a)
@@ -358,9 +373,10 @@
     key_line = chip_line(0)
     for at_hi, part in enumerate(split_halves(key_line, value_line)):
         yred[at_hi * YLO : (at_hi + 1) * YLO] = part.reshape(YLO, ZN, 8, width)
+    ysend[...] = yred[...].astype(BF16)
     for slot, (i, j) in enumerate(offsets):
         copy = pltpu.make_async_remote_copy(
-            src_ref=yred.at[(y + i) % YN, (z + j) % ZN],
+            src_ref=ysend.at[(y + i) % YN, (z + j) % ZN],
             dst_ref=precv.at[slot],
             send_sem=p_s,
             recv_sem=p_r,
@@ -370,7 +386,7 @@
         copy.start()
     pltpu.make_async_copy(precv, precv, p_r).wait()
     pltpu.make_async_copy(precv, precv, p_s).wait()
-    done = yred[y, z] + jnp.sum(precv[...], axis=0)
+    done = yred[y, z] + jnp.sum(precv[...].astype(F32), axis=0)
     out_ref[...] = done
 
 
@@ -409,12 +425,13 @@
             pltpu.VMEM((2, XN - 1, half, width), BF16),
             pltpu.VMEM((2, XN - 1, half, width), BF16),
             pltpu.VMEM((YN, ZN, 8, width), F32),
-            pltpu.VMEM((YN * ZN - 1, 8, width), F32),
+            pltpu.VMEM((YN, ZN, 8, width), BF16),
+            pltpu.VMEM((YN * ZN - 1, 8, width), BF16),
             dma((5,)),
             dma((blocks - 1,)), dma((blocks - 1,)),
             dma((2, XN)), dma((2, XN)),
             dma((2, XN - 1)), dma((2, XN - 1)),
-            pltpu.SemaphoreType.REGULAR, dma, dma,
+            *[pltpu.SemaphoreType.REGULAR] * 3, dma, dma,
         ],
         compiler_params=pltpu.CompilerParams(
             collective_id=0, has_side_effects=True, vmem_limit_bytes=56 * 2**20

time: 45.3 us -> 42.8 us (0.945)
  Pallas kernels: 43.6 us -> 41.4 us
    pallas_call x1, Pallas kernels: 43.6 us -> 41.4 us  [on_device(): pl.pallas_call(kernel, out_shape=jax.ShapeDtypeStruct((8, width), F32), i...]
where the time goes in v5:
time: 42.8 us; the launch traced here: 42.7 us
  Pallas kernels  41.4 us (97%)
  local copies, waits for them, and re-layouts  1.28 us (3%)
    pallas_call x1, Pallas kernels, on_device(): pl.pallas_call(kernel, out_shape=jax.ShapeDtypeStruct((8, width), F32), i...  41.4 us
    unnamed x1, local copies, waits for them, and re-layouts  1.28 us

profile of v5, /device:TPU:1, one launch (start us, length us, event | category | flops | bytes accessed | tf_op | source)
XLA Modules:
  0.0 42.7 jit_solution(10955254601230578515)
XLA Ops:
  0.0 41.4 %shard_map.55 = f32[8,128]{1,0:T(8,128)} custom-call(bf16[2048,128]{1,0:T(8,128)(2,1)} %bitcast.5, bf16[2048,128]{1,0:T(8,128)(2,1)} %bitcast.6, bf16[2,2048,128]{2,1,0:T(8,128)(2,1)} %cb_hbm.1, s32[2,256]{1,0:T(2,128)} %bitcast.8, s32[1,256]{1,0:T(1,128)} %bitcast.9), custom_call_target="tpu_custom_call" | custom-call | tf_op jit(solution)/shard_map/pallas_call | solution.py:399
  41.4 1.3 %copy.7 = f32[2,4,128]{2,1,0:T(4,128)} copy(f32[2,4,128]{2,1,0:T(4,128)} %bitcast.7) | data formatting | bytes 8192

commit v6 on v5

--- a/solution.py
+++ b/solution.py
@@ -105,36 +105,7 @@
     ]
     for load in loads:
         load.start()
-    grads[...] = jnp.zeros_like(grads)
-
-    tile_tok = tok // TILES
-    lanes = tile_tok * group
-    tau = lax.broadcasted_iota(jnp.int32, (1, lanes), 1) // group
-    at_tile = lax.broadcasted_iota(jnp.int32, (TILES, tok), 1) // tile_tok == lax.broadcasted_iota(
-        jnp.int32, (TILES, tok), 0
-    )
-    spread = (
-        lax.broadcasted_iota(jnp.int32, (tok, lanes), 0) % tile_tok
-        == lax.broadcasted_iota(jnp.int32, (tok, lanes), 1) // group
-    ).astype(F32).astype(BF16)
-
-    def expand(part):
-        return nn(jnp.where(at_tile, part.astype(F32), 0.0).astype(BF16), spread)
-
     loads[0].wait()
-    loads[1].wait()
-    place = seq * tok + lax.broadcasted_iota(jnp.int32, (1, tok), 1)
-    reach = jnp.minimum(reach_ref[...], place + 1)
-    reach_wide = (expand(reach // 256) * 256.0 + expand(reach % 256)).astype(jnp.int32)
-    low_ref[...] = SPAN + tau - reach_wide
-
-    loads[2].wait()
-    for table in range(2):
-        for h in range(HIGH):
-            cbt[table, h * width : (h + 1) * width, :] = cb_ref[
-                table, h * LOW : (h + 1) * LOW, :
-            ].T
-
     pl.semaphore_wait(barrier, len(greeted))
 
     id_copies = []
@@ -151,6 +122,35 @@
         id_copies.append(copy)
 
     tell(near_s, at_distance(1))
+
+    grads[...] = jnp.zeros_like(grads)
+
+    tile_tok = tok // TILES
+    lanes = tile_tok * group
+    tau = lax.broadcasted_iota(jnp.int32, (1, lanes), 1) // group
+    at_tile = lax.broadcasted_iota(jnp.int32, (TILES, tok), 1) // tile_tok == lax.broadcasted_iota(
+        jnp.int32, (TILES, tok), 0
+    )
+    spread = (
+        lax.broadcasted_iota(jnp.int32, (tok, lanes), 0) % tile_tok
+        == lax.broadcasted_iota(jnp.int32, (tok, lanes), 1) // group
+    ).astype(F32).astype(BF16)
+
+    def expand(part):
+        return nn(jnp.where(at_tile, part.astype(F32), 0.0).astype(BF16), spread)
+
+    loads[1].wait()
+    place = seq * tok + lax.broadcasted_iota(jnp.int32, (1, tok), 1)
+    reach = jnp.minimum(reach_ref[...], place + 1)
+    reach_wide = (expand(reach // 256) * 256.0 + expand(reach % 256)).astype(jnp.int32)
+    low_ref[...] = SPAN + tau - reach_wide
+
+    loads[2].wait()
+    for table in range(2):
+        for h in range(HIGH):
+            cbt[table, h * width : (h + 1) * width, :] = cb_ref[
+                table, h * LOW : (h + 1) * LOW, :
+            ].T
 
     def decode(block):
         cols = slice(block * tok, (block + 1) * tok)
@@ -331,29 +331,39 @@
         s_ref[a, own, :] = nt(rows[0, own_keys, :], q_ref[queries_of(a), :])
         d_ref[a, own, :] = nt(rows[1, own_keys, :], g_ref[queries_of(a), :])
         own_part(a)
+    pl.semaphore_wait(near_s, 4)
+    tell(two_s, at_distance(2))
     for i in range(blocks - 1):
         id_copies[i].wait()
         decode(blocks - 2 - i)
-    pl.semaphore_wait(near_s, 4)
-    tell(two_s, at_distance(2))
-
-    for a in range(TILES):
+
+    def old_scores(a):
         s_ref[a, : SPAN - a * step, :] = nt(
             rows[0, a * step : SPAN, :], q_ref[queries_of(a), :]
         )
+
+    def old_dots(a):
+        d_ref[a, : SPAN - a * step, :] = nt(
+            rows[1, a * step : SPAN, :], g_ref[queries_of(a), :]
+        )
+
+    old_scores(0)
+    for a in range(TILES):
+        if a < TILES - 1:
+            old_scores(a + 1)
         if a > 0:
             add_values(a - 1)
         softmax(a)
     add_values(TILES - 1)
     pl.semaphore_wait(two_s, 4)
     tell(line_s, y_peers)
+    old_dots(0)
     for flip in (1, 0):
         scatter(1, flip)
         to_buddy(1, flip)
     for a in range(TILES):
-        d_ref[a, : SPAN - a * step, :] = nt(
-            rows[1, a * step : SPAN, :], g_ref[queries_of(a), :]
-        )
+        if a < TILES - 1:
+            old_dots(a + 1)
         if a > 0:
             add_keys(a - 1)
         if a == 2:

time: 42.8 us -> 42.4 us (level)
  Pallas kernels: 41.4 us -> 40.9 us
    pallas_call x1, Pallas kernels: 41.4 us -> 40.9 us  [on_device(): pl.pallas_call(kernel, out_shape=jax.ShapeDtypeStruct((8, width), F32), i...]
where the time goes in v6:
time: 42.4 us; the launch traced here: 42.2 us
  Pallas kernels  40.9 us (96%)
  local copies, waits for them, and re-layouts  1.28 us (3%)
    pallas_call x1, Pallas kernels, on_device(): pl.pallas_call(kernel, out_shape=jax.ShapeDtypeStruct((8, width), F32), i...  40.9 us
    unnamed x1, local copies, waits for them, and re-layouts  1.28 us

profile of v6, /device:TPU:1, one launch (start us, length us, event | category | flops | bytes accessed | tf_op | source)
XLA Modules:
  0.0 42.2 jit_solution(9431971762239116546)
XLA Ops:
  0.0 40.9 %shard_map.55 = f32[8,128]{1,0:T(8,128)} custom-call(bf16[2048,128]{1,0:T(8,128)(2,1)} %bitcast.5, bf16[2048,128]{1,0:T(8,128)(2,1)} %bitcast.6, bf16[2,2048,128]{2,1,0:T(8,128)(2,1)} %cb_hbm.1, s32[2,256]{1,0:T(2,128)} %bitcast.8, s32[1,256]{1,0:T(1,128)} %bitcast.9), custom_call_target="tpu_custom_call" | custom-call | tf_op jit(solution)/shard_map/pallas_call | solution.py:409
  41.0 1.3 %copy.7 = f32[2,4,128]{2,1,0:T(4,128)} copy(f32[2,4,128]{2,1,0:T(4,128)} %bitcast.7) | data formatting | bytes 8192
